TPU v7x, 32 devices: a whole 2x2x4 slice. The times are simulated.
32 devices in a mesh: row: 8 (over z, y), col: 4 (over x, core).
Axes of the slice: x: 2, y: 2, z: 4, core: 2. Of those that a mesh axis runs over, the one named last changes fastest.
Arguments:
- covariance: float32 [16384, 16384], P('row', 'col'), as said below
- courant: float32 [2, 16384], replicated, may hold values from 0.05 to 0.45
- upwind: int32 [16384], replicated, may hold values from 0 to 3
- observed: int32 [2, 256], replicated, may hold values from 0 to 16383
- noise: float32 [2, 256], replicated, may hold values from 0.5 to 2
Outputs:
- posterior: float32 [16384, 16384], P('row', 'col')
Inputs may be any that keep to these rules, and one draw needn't show every extreme that they name: The covariance is symmetric and positive definite.
All inputs are finite; a program needn't handle non-finite values.
Results may differ from a plain program's by a relative error of at most 0.0003.
Values sent between devices are 32-bit elements; how exact they have to be, the bound alone decides.
A program may use at most 256 MiB of HBM per device.

v0:
```python
import jax
import jax.numpy as jnp
from jax import lax
from jax.sharding import PartitionSpec as P

G = 128
BATCHES = 2


def extended(block, sides, width):
    for axis, dim in sides:
        count = lax.axis_size(axis)
        forward = [(i, i + 1) for i in range(count - 1)]
        backward = [(target, source) for source, target in forward]
        low = lax.ppermute(
            lax.slice_in_dim(block, block.shape[dim] - width, None, axis=dim), axis, forward
        )
        high = lax.ppermute(lax.slice_in_dim(block, 0, width, axis=dim), axis, backward)
        block = jnp.concatenate([low, block, high], axis=dim)
    return block


def left_apply(padded, cour_a, cour_b, up_dir):
    lines = padded.shape[0] - 2
    center = padded[1:-1]
    prev_line = padded[:-2]
    next_line = padded[2:]
    prev_cell = jnp.pad(center, ((0, 0), (1, 0), (0, 0)))[:, :-1]
    next_cell = jnp.pad(center, ((0, 0), (0, 1), (0, 0)))[:, 1:]
    coef_a = cour_a.reshape(lines, G, 1)
    coef_b = cour_b.reshape(lines, G, 1)
    dirs = up_dir.reshape(lines, G, 1)
    up_line = jnp.where(dirs % 2 == 1, next_line, prev_line)
    up_cell = jnp.where(dirs // 2 == 1, next_cell, prev_cell)
    return (1.0 - coef_a - coef_b) * center + coef_a * up_line + coef_b * up_cell


def right_apply(padded, cour_a, cour_b, up_dir):
    lines = padded.shape[1] - 2
    center = padded[:, 1:-1]
    prev_line = padded[:, :-2]
    next_line = padded[:, 2:]
    prev_cell = jnp.pad(center, ((0, 0), (0, 0), (1, 0)))[:, :, :-1]
    next_cell = jnp.pad(center, ((0, 0), (0, 0), (0, 1)))[:, :, 1:]
    coef_a = cour_a.reshape(1, lines, G)
    coef_b = cour_b.reshape(1, lines, G)
    dirs = up_dir.reshape(1, lines, G)
    up_line = jnp.where(dirs % 2 == 1, next_line, prev_line)
    up_cell = jnp.where(dirs // 2 == 1, next_cell, prev_cell)
    return (1.0 - coef_a - coef_b) * center + coef_a * up_line + coef_b * up_cell


def transport(block, row_cour, row_dirs, col_cour, col_dirs):
    row_count, col_count = block.shape
    padded = extended(block, (("row", 0),), G)
    padded = padded.reshape(row_count // G + 2, G, col_count)
    block = left_apply(padded, row_cour[0], row_cour[1], row_dirs).reshape(row_count, col_count)
    padded = extended(block, (("col", 1),), G)
    padded = padded.reshape(row_count, col_count // G + 2, G)
    return right_apply(padded, col_cour[0], col_cour[1], col_dirs).reshape(row_count, col_count)


def shards(covariance, courant, upwind, observed, noise):
    row_count, col_count = covariance.shape
    row_start = lax.axis_index("row") * row_count
    col_start = lax.axis_index("col") * col_count
    row_cour = lax.dynamic_slice_in_dim(courant, row_start, row_count, 1)
    col_cour = lax.dynamic_slice_in_dim(courant, col_start, col_count, 1)
    row_dirs = lax.dynamic_slice_in_dim(upwind, row_start, row_count, 0)
    col_dirs = lax.dynamic_slice_in_dim(upwind, col_start, col_count, 0)
    block = covariance
    for cycle in range(BATCHES):
        block = transport(block, row_cour, row_dirs, col_cour, col_dirs)
        obs = observed[cycle]
        local_rows = obs - row_start
        owns_row = (local_rows >= 0) & (local_rows < row_count)
        row_pick = jnp.clip(local_rows, 0, row_count - 1)
        local_cols = obs - col_start
        owns_col = (local_cols >= 0) & (local_cols < col_count)
        col_pick = jnp.clip(local_cols, 0, col_count - 1)
        row_part = jnp.where(owns_row[:, None], jnp.take(block, row_pick, axis=0), 0.0)
        col_part = jnp.where(owns_col[None, :], jnp.take(block, col_pick, axis=1), 0.0)
        row_panel = lax.psum(row_part, "row")
        block_part = jnp.where(owns_col[None, :], jnp.take(row_panel, col_pick, axis=1), 0.0)
        col_panel, innov = lax.psum((col_part, block_part), "col")
        innov = innov + jnp.diag(noise[cycle])
        factor = jnp.linalg.cholesky(innov)
        gain = jax.scipy.linalg.cho_solve((factor, True), col_panel.T).T
        block = block - jnp.dot(
            gain, row_panel, precision=lax.Precision.HIGHEST, preferred_element_type=jnp.float32
        )
    return block


def solution(mesh):
    in_specs = (P("row", "col"), P(), P(), P(), P())
    out_specs = P("row", "col")
    return jax.shard_map(shards, mesh=mesh, in_specs=in_specs, out_specs=out_specs, check_vma=False)
```

profile of v0, /device:TPU:0, one launch (start us, length us, event | category | flops | bytes accessed | tf_op | source)
XLA Modules:
  0.0 1521.9 jit_solution(16058339362383866526)
XLA Ops:
  24.9 37.1 %collective-permute-done = f32[128,4096]{1,0:T(8,128)S(1)} collective-permute-done((f32[128,4096]{1,0:T(8,128)}, f32[128,4096]{1,0:T(8,128)S(1)}, u32[]{:S(2)}, u32[]{:S(2)}) %collective-permute-start) | collective-permute-done | bytes 2097184 | tf_op jit(solution)/shard_map/ppermute | solution.py:18
  62.0 45.2 %collective-permute-done.1 = f32[128,4096]{1,0:T(8,128)} collective-permute-done((f32[128,4096]{1,0:T(8,128)}, f32[128,4096]{1,0:T(8,128)}, u32[]{:S(2)}, u32[]{:S(2)}) %collective-permute-start.1) | collective-permute-done | bytes 2097184 | tf_op jit(solution)/shard_map/ppermute | solution.py:15
  107.2 41.7 %pad_maximum_fusion.4 = (f32[2048,4096]{1,0:T(8,128)}, f32[2048,4096]{1,0:T(8,128)}) fusion(f32[2048,4096]{1,0:T(8,128)} %param.14, f32[128,4096]{1,0:T(8,128)} %collective-permute-done.1, f32[128,4096]{1,0:T(8,128)S(1)} %collective-permute-done), kind=kLoop, calls=%fused_computation.40 | loop fusion | flops 16777216 | bytes 104857600 | tf_op jit(solution)/shard_map/concatenate | solution.py:19
  148.9 67.2 %fusion.2 = f32[16,128,4096]{2,1,0:T(8,128)} fusion(f32[16,128,4096]{2,1,0:T(8,128)} %bitcast.163, f32[16,128,4096]{2,1,0:T(8,128)} %bitcast.167, f32[16,128,4096]{2,1,0:T(8,128)} %bitcast.166, f32[16,128]{1,0:T(8,128)S(1)} %bitcast.180, f32[16,128]{1,0:T(8,128)S(1)} %bitcast.177, f32[16,128]{1,0:T(8,128)S(1)} %subtract_subtract_fusion.1, ...), kind=kLoop, calls=%fused_computation.22 | loop fusion | flops 58720256 | bytes 134246400 | tf_op jit(solution)/shard_map/add | solution.py:35
  216.2 33.4 %copy.22 = f32[2048,4096]{0,1:T(8,128)} copy(f32[2048,4096]{1,0:T(8,128)} %bitcast.169) | data formatting | bytes 67108864 | tf_op jit(solution)/shard_map/reshape | solution.py:57
  258.8 23.4 %pad_maximum_fusion = f32[2048,4352]{0,1:T(8,128)} fusion(f32[2048,128]{0,1:T(8,128)S(1)} %collective-permute-done.3, f32[2048,4096]{0,1:T(8,128)} %copy.22, f32[2048,128]{0,1:T(8,128)S(1)} %collective-permute-done.2), kind=kLoop, calls=%fused_computation.10 | loop fusion | flops 17825792 | bytes 71303168 | tf_op jit(solution)/shard_map/concatenate | solution.py:19
  282.2 23.2 %slice.240 = f32[2048,32,128]{0,2,1:T(8,128)} slice(f32[2048,34,128]{0,2,1:T(8,128)} %bitcast.156), slice={[0:2048], [1:33], [0:128]} | slice | bytes 67108864 | tf_op jit(solution)/shard_map/slice | solution.py:40
  305.4 65.4 %fusion.5 = f32[2048,32,128]{0,2,1:T(8,128)} fusion(f32[2048,32,128]{0,2,1:T(8,128)} %slice.240, f32[2048,34,128]{0,2,1:T(8,128)} %bitcast.157, f32[32,128]{1,0:T(8,128)S(1)} %bitcast.174, f32[32,128]{1,0:T(8,128)S(1)} %bitcast.171, f32[32,128]{1,0:T(8,128)S(1)} %subtract_subtract_fusion, pred[32,128]{1,0:T(8,128)(4,1)S(1)} %fusion.47, ...), kind=kLoop, calls=%fused_computation.25 | loop fusion | flops 58720256 | bytes 134275072 | tf_op jit(solution)/shard_map/add | solution.py:50
  370.8 31.1 %copy.23 = f32[2048,4096]{1,0:T(8,128)} copy(f32[2048,4096]{0,1:T(8,128)} %bitcast.161) | data formatting | bytes 67108864 | tf_op jit(solution)/shard_map/reshape | solution.py:60
  438.0 153.7 %all-reduce.16.cloned.1.call-done = f32[256,4096]{1,0:T(8,128)} async-done(((f32[256,4096]{1,0:T(8,128)}), f32[256,4096]{1,0:T(8,128)}) %all-reduce.16.cloned.1.call-update) | async-done | bytes 4194320 | tf_op jit(solution)/shard_map/psum | solution.py:83
  602.3 54.2 %all-reduce.22.cloned.1.call-done = (f32[256,2048]{1,0:T(8,128)}, f32[256,256]{0,1:T(8,128)}) async-done(((f32[256,2048]{1,0:T(8,128)}, f32[256,256]{0,1:T(8,128)}), (f32[256,2048]{1,0:T(8,128)}, f32[256,256]{0,1:T(8,128)})) %all-reduce.22.cloned.1.call-update) | async-done | bytes 2359312 | tf_op jit(solution)/shard_map/psum | solution.py:85
  728.4 35.2 %convolution_subtract_fusion.1 = f32[2048,4096]{1,0:T(8,128)} fusion(f32[2048,4096]{1,0:T(8,128)} %copy.23, f32[256,4096]{1,0:T(8,128)} %all-reduce.16.cloned.1.call-done, f32[128,2048]{1,0:T(8,128)S(1)} %fusion.37, f32[128,2048]{1,0:T(8,128)S(1)} %fusion.36), kind=kOutput, calls=%fused_computation.43 | convolution fusion | flops 25778716672 | bytes 73400320 | tf_op jit(solution)/shard_map/dot_general | solution.py:89
  772.2 43.2 %collective-permute-done.4 = f32[128,4096]{1,0:T(8,128)S(1)} collective-permute-done((f32[128,4096]{1,0:T(8,128)S(1)}, f32[128,4096]{1,0:T(8,128)S(1)}, u32[]{:S(2)}, u32[]{:S(2)}) %collective-permute-start.4) | collective-permute-done | bytes 2097184 | tf_op jit(solution)/shard_map/ppermute | solution.py:18
  815.3 44.8 %collective-permute-done.5 = f32[128,4096]{1,0:T(8,128)S(1)} collective-permute-done((f32[128,4096]{1,0:T(8,128)S(1)}, f32[128,4096]{1,0:T(8,128)S(1)}, u32[]{:S(2)}, u32[]{:S(2)}) %collective-permute-start.5) | collective-permute-done | bytes 2097184 | tf_op jit(solution)/shard_map/ppermute | solution.py:15
  860.2 41.4 %pad_maximum_fusion.2 = (f32[2048,4096]{1,0:T(8,128)}, f32[2048,4096]{1,0:T(8,128)}) fusion(f32[2048,4096]{1,0:T(8,128)} %convolution_subtract_fusion.1, f32[128,4096]{1,0:T(8,128)S(1)} %collective-permute-done.5, f32[128,4096]{1,0:T(8,128)S(1)} %collective-permute-done.4), kind=kLoop, calls=%fused_computation.35 | loop fusion | flops 16777216 | bytes 104857600 | tf_op jit(solution)/shard_map/concatenate | solution.py:19
  901.6 67.0 %fusion.8 = f32[16,128,4096]{2,1,0:T(8,128)} fusion(f32[16,128,4096]{2,1,0:T(8,128)} %bitcast.158, f32[16,128,4096]{2,1,0:T(8,128)} %bitcast.165, f32[16,128,4096]{2,1,0:T(8,128)} %bitcast.164, f32[16,128]{1,0:T(8,128)S(1)} %bitcast.181, f32[16,128]{1,0:T(8,128)S(1)} %bitcast.178, f32[16,128]{1,0:T(8,128)S(1)} %copy-done.11, ...), kind=kLoop, calls=%fused_computation.28 | loop fusion | flops 58720256 | bytes 134246400 | tf_op jit(solution)/shard_map/add | solution.py:35
  968.6 33.3 %copy.24 = f32[2048,4096]{0,1:T(8,128)} copy(f32[2048,4096]{1,0:T(8,128)} %bitcast.168) | data formatting | bytes 67108864 | tf_op jit(solution)/shard_map/reshape | solution.py:57
  1010.5 23.6 %pad_maximum_fusion.1 = f32[2048,4352]{0,1:T(8,128)} fusion(f32[2048,128]{0,1:T(8,128)S(1)} %collective-permute-done.7, f32[2048,4096]{0,1:T(8,128)} %copy.24, f32[2048,128]{0,1:T(8,128)S(1)} %collective-permute-done.6), kind=kLoop, calls=%fused_computation.11 | loop fusion | flops 17825792 | bytes 71303168 | tf_op jit(solution)/shard_map/concatenate | solution.py:19
  1034.2 23.2 %slice.247 = f32[2048,32,128]{0,2,1:T(8,128)} slice(f32[2048,34,128]{0,2,1:T(8,128)} %bitcast.154), slice={[0:2048], [1:33], [0:128]} | slice | bytes 67108864 | tf_op jit(solution)/shard_map/slice | solution.py:40
  1057.4 65.4 %fusion.11 = f32[2048,32,128]{0,2,1:T(8,128)} fusion(f32[2048,32,128]{0,2,1:T(8,128)} %slice.247, f32[2048,34,128]{0,2,1:T(8,128)} %bitcast.155, f32[32,128]{1,0:T(8,128)S(1)} %bitcast.175, f32[32,128]{1,0:T(8,128)S(1)} %bitcast.172, f32[32,128]{1,0:T(8,128)S(1)} %copy-done.5, pred[32,128]{1,0:T(8,128)(4,1)S(1)} %copy-done.15, pred[32,128]{1,0:T(8,128)(4,1)S(1)} %copy-done.13), kind=kLoop, calls=%fused_computation.31 | loop fusion | flops 58720256 | bytes 134275072 | tf_op jit(solution)/shard_map/add | solution.py:50
  1122.8 31.1 %copy.25 = f32[2048,4096]{1,0:T(8,128)} copy(f32[2048,4096]{0,1:T(8,128)} %bitcast.159) | data formatting | bytes 67108864 | tf_op jit(solution)/shard_map/reshape | solution.py:60
  1190.0 153.5 %all-reduce.18.cloned.1.call-done = f32[256,4096]{1,0:T(8,128)} async-done(((f32[256,4096]{1,0:T(8,128)}), f32[256,4096]{1,0:T(8,128)}) %all-reduce.18.cloned.1.call-update) | async-done | bytes 4194320 | tf_op jit(solution)/shard_map/psum | solution.py:83
  1353.7 55.0 %all-reduce.20.cloned.1.call-done = (f32[256,2048]{1,0:T(8,128)}, f32[256,256]{0,1:T(8,128)}) async-done(((f32[256,2048]{1,0:T(8,128)}, f32[256,256]{0,1:T(8,128)}), (f32[256,2048]{1,0:T(8,128)}, f32[256,256]{0,1:T(8,128)})) %all-reduce.20.cloned.1.call-update) | async-done | bytes 2359312 | tf_op jit(solution)/shard_map/psum | solution.py:85
  1479.9 35.3 %convolution_subtract_fusion = f32[2048,4096]{1,0:T(8,128)} fusion(f32[2048,4096]{1,0:T(8,128)} %copy.25, f32[256,4096]{1,0:T(8,128)} %all-reduce.18.cloned.1.call-done, f32[128,2048]{1,0:T(8,128)S(1)} %fusion.40, f32[128,2048]{1,0:T(8,128)S(1)} %fusion.39), kind=kOutput, calls=%fused_computation.42 | convolution fusion | flops 25778716672 | bytes 73400320 | tf_op jit(solution)/shard_map/dot_general | solution.py:89
  (185 shorter events, 285.5 us)
Async XLA Ops:
  6.5 585.2 %all-reduce.16.cloned.1.call-start = ((), (), s32[]{:S(2)}) async-start(), calls=%async_computation | async-start | bytes 8388608 | tf_op jit(solution)/shard_map/psum | solution.py:83
  11.3 50.7 %collective-permute-start = (f32[128,4096]{1,0:T(8,128)}, f32[128,4096]{1,0:T(8,128)S(1)}, u32[]{:S(2)}, u32[]{:S(2)}) collective-permute-start(f32[128,4096]{1,0:T(8,128)} %get-tuple-element.69), channel_id=1, source_target_pairs={{4,0},{8,4},{12,8},{16,12},{20,16},{24,20},{28,24},{5,1},{9,5},{13... | collective-permute-start | bytes 6291464 | tf_op jit(solution)/shard_map/ppermute | solution.py:18
  12.5 94.6 %collective-permute-start.1 = (f32[128,4096]{1,0:T(8,128)}, f32[128,4096]{1,0:T(8,128)}, u32[]{:S(2)}, u32[]{:S(2)}) collective-permute-start(f32[128,4096]{1,0:T(8,128)} %get-tuple-element.68), channel_id=1, source_target_pairs={{0,4},{4,8},{8,12},{12,16},{16,20},{20,24},{24,28},{1,5},{5,9},{9,... | collective-permute-start | bytes 6291464 | tf_op jit(solution)/shard_map/ppermute | solution.py:15
  20.1 128.8 %copy-start.16 = (pred[16,128]{1,0:T(8,128)(4,1)}, pred[16,128]{1,0:T(8,128)(4,1)S(1)}, u32[]{:S(2)}) copy-start(pred[16,128]{1,0:T(8,128)(4,1)S(1)} %get-tuple-element.52) | copy-start | bytes 6148
  20.8 284.6 %copy-start.12 = (pred[32,128]{1,0:T(8,128)(4,1)}, pred[32,128]{1,0:T(8,128)(4,1)S(1)}, u32[]{:S(2)}) copy-start(pred[32,128]{1,0:T(8,128)(4,1)S(1)} %get-tuple-element.50) | copy-start | bytes 12292
  23.9 125.0 %copy-start.18 = (pred[16,128]{1,0:T(8,128)(4,1)}, pred[16,128]{1,0:T(8,128)(4,1)S(1)}, u32[]{:S(2)}) copy-start(pred[16,128]{1,0:T(8,128)(4,1)S(1)} %fusion.52) | copy-start | bytes 6148
  24.8 124.1 %copy-start.8 = (f32[1,2048]{1,0:T(1,128)}, f32[1,2048]{1,0:T(1,128)S(1)}, u32[]{:S(2)}) copy-start(f32[1,2048]{1,0:T(1,128)S(1)} %get-tuple-element.73) | copy-start | bytes 24580
  251.2 5.8 collective-permute-start.2
  253.2 5.6 collective-permute-start.3
  418.2 183.6 %copy-start.29 = (f32[2,256]{1,0:T(2,128)S(1)}, f32[2,256]{1,0:T(2,128)}, u32[]{:S(2)}) copy-start(f32[2,256]{1,0:T(2,128)} %param.18) | copy-start | bytes 6148
  423.3 233.2 %all-reduce.22.cloned.1.call-start = ((), (), s32[]{:S(2)}) async-start(), calls=%async_computation.3 | async-start | bytes 4718592 | tf_op jit(solution)/shard_map/psum | solution.py:85
  601.5 742.1 %all-reduce.18.cloned.1.call-start = ((), (), s32[]{:S(2)}) async-start(), calls=%async_computation.1 | async-start | bytes 8388608 | tf_op jit(solution)/shard_map/psum | solution.py:83
  766.1 49.2 %collective-permute-start.4 = (f32[128,4096]{1,0:T(8,128)S(1)}, f32[128,4096]{1,0:T(8,128)S(1)}, u32[]{:S(2)}, u32[]{:S(2)}) collective-permute-start(f32[128,4096]{1,0:T(8,128)S(1)} %get-tuple-element.63), channel_id=1, source_target_pairs={{4,0},{8,4},{12,8},{16,12},{20,16},{24,20},{28,24},{5,1},{9,5},{13... | collective-permute-start | bytes 6291464 | tf_op jit(solution)/shard_map/ppermute | solution.py:18
  767.4 134.2 %copy-start.7 = (f32[1,2048]{1,0:T(1,128)S(1)}, f32[1,2048]{1,0:T(1,128)}, u32[]{:S(2)}) copy-start(f32[1,2048]{1,0:T(1,128)} %copy-done.6) | copy-start | bytes 24580
  767.4 134.2 %copy-start.9 = (f32[1,2048]{1,0:T(1,128)S(1)}, f32[1,2048]{1,0:T(1,128)}, u32[]{:S(2)}) copy-start(f32[1,2048]{1,0:T(1,128)} %copy-done.8) | copy-start | bytes 24580
  767.5 134.1 %copy-start.11 = (f32[16,128]{1,0:T(8,128)S(1)}, f32[16,128]{1,0:T(8,128)}, u32[]{:S(2)}) copy-start(f32[16,128]{1,0:T(8,128)} %copy-done.10) | copy-start | bytes 24580
  767.5 134.1 %copy-start.17 = (pred[16,128]{1,0:T(8,128)(4,1)S(1)}, pred[16,128]{1,0:T(8,128)(4,1)}, u32[]{:S(2)}) copy-start(pred[16,128]{1,0:T(8,128)(4,1)} %copy-done.16) | copy-start | bytes 6148
  767.5 134.1 %copy-start.19 = (pred[16,128]{1,0:T(8,128)(4,1)S(1)}, pred[16,128]{1,0:T(8,128)(4,1)}, u32[]{:S(2)}) copy-start(pred[16,128]{1,0:T(8,128)(4,1)} %copy-done.18) | copy-start | bytes 6148
  767.5 92.7 %collective-permute-start.5 = (f32[128,4096]{1,0:T(8,128)S(1)}, f32[128,4096]{1,0:T(8,128)S(1)}, u32[]{:S(2)}, u32[]{:S(2)}) collective-permute-start(f32[128,4096]{1,0:T(8,128)S(1)} %get-tuple-element.62), channel_id=1, source_target_pairs={{0,4},{4,8},{8,12},{12,16},{16,20},{20,24},{24,28},{1,5},{5,9},{9,... | collective-permute-start | bytes 6291464 | tf_op jit(solution)/shard_map/ppermute | solution.py:15
  1003.7 4.2 collective-permute-start.6
  1005.7 4.9 collective-permute-start.7
  1170.1 238.6 %copy-start.20 = (f32[1,256]{1,0:T(1,128)S(1)}, f32[1,256]{1,0:T(1,128)}, u32[]{:S(2)}) copy-start(f32[1,256]{1,0:T(1,128)} %get-tuple-element.82) | copy-start | bytes 3076
  1170.1 277.2 %copy-start.31 = (s32[2,2]{1,0:T(2,128)S(1)}, s32[2,2]{1,0:T(2,128)}, u32[]{:S(2)}) copy-start(s32[2,2]{1,0:T(2,128)} %copy-done.30) | copy-start | bytes 52
  1175.3 233.4 %all-reduce.20.cloned.1.call-start = ((), (), s32[]{:S(2)}) async-start(), calls=%async_computation.2 | async-start | bytes 4718592 | tf_op jit(solution)/shard_map/psum | solution.py:85
  (20 other events, 762.1 us)
Sparse Core Ops, SparseCore 0:
  423.4 168.2 all-reduce.15
  601.6 54.8 all-reduce.21
  1175.4 168.0 all-reduce.17
  1353.8 54.8 all-reduce.19
where the time goes:
time: 1530 us; the launch traced here: 1520 us
  waiting for transfers between devices  592 us (39%)
  other arithmetic  529 us (35%)
  local copies, waits for them, and re-layouts  274 us (18%)
  matrix products  88.7 us (6%)
  starting transfers between devices  21.2 us (1%)
  between operations  16.7 us (1%)
    psum x2, waiting for transfers between devices, shards(): row_panel = lax.psum(row_part, 'row')  307 us
    add x2, other arithmetic, left_apply(): (1.0 - coef_a - coef_b) * center + coef_a * up_line + coef_b * up_cell  134 us
    add x2, other arithmetic, right_apply(): (1.0 - coef_a - coef_b) * center + coef_a * up_line + coef_b * up_cell  131 us
    concatenate x4, other arithmetic, extended(): block = jnp.concatenate([low, block, high], axis=dim)  130 us
    psum x2, waiting for transfers between devices, shards(): col_panel, innov = lax.psum((col_part, block_part), 'col')  109 us
    ppermute x4, waiting for transfers between devices, extended(): lax.ppermute(lax.slice_in_dim(block, block.shape[dim] - width, None, axis...  90.9 us
    ppermute x4, waiting for transfers between devices, extended(): lax.ppermute(lax.slice_in_dim(block, 0, width, axis=dim), axis, backward)  84.6 us
    dot_general x2, matrix products, shards(): jnp.dot(gain, row_panel, precision=lax.Precision.HIGHEST, preferred_eleme...  70.5 us
  transfers between devices with their start and end apart: 12, of which 11 were waited for; matrix products, arithmetic and copies ran while one was open for 2% of the time, Pallas kernels for 0%

commit v1 on v0

v1 whole, which is shorter than its diff:
```python
import functools
import math

import jax
import jax.numpy as jnp
from jax import lax
from jax.experimental import pallas as pl
from jax.experimental.pallas import tpu as pltpu
from jax.sharding import PartitionSpec as P

VMEM_BYTES = 56 * 2**20
HIGHEST = lax.Precision.HIGHEST


def shifted(block, axis, dim, width):
    count = lax.axis_size(axis)
    forward = [(i, i + 1) for i in range(count - 1)]
    backward = [(target, source) for source, target in forward]
    size = block.shape[dim]
    low = lax.ppermute(lax.slice_in_dim(block, size - width, size, axis=dim), axis, forward)
    high = lax.ppermute(lax.slice_in_dim(block, 0, width, axis=dim), axis, backward)
    return low, high


def stencil(coefs, prev, center, following, axis, side):
    out = coefs[0] * center + coefs[1] * prev + coefs[2] * following
    out = out + coefs[3] * pltpu.roll(center, 1, axis)
    return out + coefs[4] * pltpu.roll(center, side - 1, axis)


def each_line(first, last, group, body):
    rounds = (last - first) // group

    @pl.loop(0, rounds)
    def _(turn):
        for place in range(group):
            body(first + turn * group + place)

    for line in range(first + rounds * group, last):
        body(line)


def sweep(side, lines, low, middle, high, coefs_at, half, store, axis, group):
    def first(line, prev, center, following):
        half(line + 1, stencil(coefs_at(line + 1), prev, center, following, axis, side))

    first(-1, low(0), low(1), middle(0))
    first(0, low(1), middle(0), middle(1))

    each_line(
        1,
        lines - 1,
        group,
        lambda line: first(line, middle(line - 1), middle(line), middle(line + 1)),
    )
    first(lines - 1, middle(lines - 2), middle(lines - 1), high(0))
    first(lines, middle(lines - 1), high(0), high(1))

    def second(line):
        out = stencil(coefs_at(line + 1), half(line), half(line + 1), half(line + 2), axis, side)
        store(line, out)

    each_line(0, lines, group, second)


def start_of(line, side):
    return pl.ds(line * side if isinstance(line, int) else pl.multiple_of(line * side, side), side)


def left_kernel(side, low_ref, mid_ref, high_ref, coef_ref, out_ref, half_ref):
    rows, width = mid_ref.shape
    lanes = coef_ref.shape[2]
    for piece in range(width // lanes):
        cols = pl.ds(piece * lanes, lanes)

        def read(ref):
            return lambda line: ref[start_of(line, side), cols]

        def half(line, value=None):
            if value is None:
                return half_ref[start_of(line, side), cols]
            half_ref[start_of(line, side), cols] = value

        def store(line, value):
            out_ref[start_of(line, side), cols] = value

        def coefs_at(line):
            return [coef_ref[k, start_of(line, side), :] for k in range(5)]

        sweep(side, rows // side, read(low_ref), read(mid_ref), read(high_ref), coefs_at, half, store, 0, 1)


def right_kernel(side, low_ref, mid_ref, high_ref, coef_ref, out_ref, half_ref):
    rows, width = mid_ref.shape
    copies = rows // coef_ref.shape[1]

    def read(ref):
        return lambda line: ref[:, start_of(line, side)]

    def half(line, value=None):
        if value is None:
            return half_ref[:, start_of(line, side)]
        half_ref[:, start_of(line, side)] = value

    def store(line, value):
        out_ref[:, start_of(line, side)] = value

    def coefs_at(line):
        return [
            jnp.concatenate([coef_ref[k, :, start_of(line, side)]] * copies, axis=0)
            for k in range(5)
        ]

    sweep(side, width // side, read(low_ref), read(mid_ref), read(high_ref), coefs_at, half, store, 1, 3)


def left_twice(low, block, high, coefs, side):
    rows, width = block.shape
    tile = min(256, width)
    lanes = 128
    spread = jnp.broadcast_to(coefs[:, :, None], (*coefs.shape, lanes))

    def spec(count):
        return pl.BlockSpec((count, tile), lambda i: (0, i))

    return pl.pallas_call(
        functools.partial(left_kernel, side),
        grid=(width // tile,),
        in_specs=[
            spec(2 * side),
            spec(rows),
            spec(2 * side),
            pl.BlockSpec(spread.shape, lambda i: (0, 0, 0)),
        ],
        out_specs=spec(rows),
        out_shape=jax.ShapeDtypeStruct(block.shape, block.dtype),
        scratch_shapes=[pltpu.VMEM((rows + 2 * side, tile), block.dtype)],
        compiler_params=pltpu.CompilerParams(vmem_limit_bytes=VMEM_BYTES),
        cost_estimate=pl.CostEstimate(
            flops=36 * rows * width, bytes_accessed=8 * rows * width, transcendentals=0
        ),
    )(low, block, high, spread)


def right_twice(low, block, high, coefs, side):
    rows, width = block.shape
    tile = min(128, rows)
    spread = jnp.broadcast_to(coefs[:, None, :], (coefs.shape[0], 8, coefs.shape[1]))

    def spec(count):
        return pl.BlockSpec((tile, count), lambda i: (i, 0))

    return pl.pallas_call(
        functools.partial(right_kernel, side),
        grid=(rows // tile,),
        in_specs=[
            spec(2 * side),
            spec(width),
            spec(2 * side),
            pl.BlockSpec(spread.shape, lambda i: (0, 0, 0)),
        ],
        out_specs=spec(width),
        out_shape=jax.ShapeDtypeStruct(block.shape, block.dtype),
        scratch_shapes=[pltpu.VMEM((tile, width + 2 * side), block.dtype)],
        compiler_params=pltpu.CompilerParams(vmem_limit_bytes=VMEM_BYTES),
        cost_estimate=pl.CostEstimate(
            flops=36 * rows * width, bytes_accessed=8 * rows * width, transcendentals=0
        ),
    )(low, block, high, spread)


def subtract_kernel(tile, block_ref, left_ref, right_ref, out_ref):
    @pl.loop(0, block_ref.shape[1] // tile)
    def _(turn):
        cols = pl.ds(pl.multiple_of(turn * tile, tile), tile)
        product = jnp.dot(
            left_ref[...],
            right_ref[:, cols],
            precision=HIGHEST,
            preferred_element_type=jnp.float32,
        )
        out_ref[:, cols] = block_ref[:, cols] - product


def subtract_product(block, left, right):
    rows, width = block.shape
    depth = left.shape[1]
    tile = min(256, rows)

    def strip(count):
        return pl.BlockSpec((tile, count), lambda i: (i, 0))

    return pl.pallas_call(
        functools.partial(subtract_kernel, min(512, width)),
        grid=(rows // tile,),
        in_specs=[strip(width), strip(depth), pl.BlockSpec((depth, width), lambda i: (0, 0))],
        out_specs=strip(width),
        out_shape=jax.ShapeDtypeStruct(block.shape, block.dtype),
        compiler_params=pltpu.CompilerParams(vmem_limit_bytes=VMEM_BYTES),
        cost_estimate=pl.CostEstimate(
            flops=12 * rows * width * depth, bytes_accessed=8 * rows * width, transcendentals=0
        ),
    )(block, left, right)


def stencil_coefs(courant, upwind, side):
    total = upwind.shape[0]
    place = jnp.arange(total) % side
    frac_a, frac_b = courant[0], courant[1]
    next_line, next_cell = upwind % 2 == 1, upwind // 2 == 1
    coefs = jnp.stack(
        [
            1.0 - frac_a - frac_b,
            jnp.where(next_line, 0.0, frac_a),
            jnp.where(next_line, frac_a, 0.0),
            jnp.where(next_cell | (place == 0), 0.0, frac_b),
            jnp.where(next_cell & (place != side - 1), frac_b, 0.0),
        ]
    )
    return jnp.pad(coefs, ((0, 0), (side, side)))


def expand(index, value, table, side):
    total = table.shape[1]
    frac_a, frac_b, dirs = jnp.take(table, index.reshape(-1), axis=1).reshape(3, *index.shape)
    next_cell = dirs >= 2.0
    next_line = (dirs == 1.0) | (dirs == 3.0)
    line = index + jnp.where(next_line, side, -side)
    step = jnp.where(next_cell, 1, -1)
    place = index % side + step
    line_ok = (line >= 0) & (line < total)
    cell_ok = (place >= 0) & (place < side)
    indices = [index, jnp.clip(line, 0, total - 1), jnp.clip(index + step, 0, total - 1)]
    values = [
        value * (1.0 - frac_a - frac_b),
        jnp.where(line_ok, value * frac_a, 0.0),
        jnp.where(cell_ok, value * frac_b, 0.0),
    ]
    return jnp.concatenate(indices), jnp.concatenate(values)


def dense(terms, start, count):
    cells = start + jnp.arange(count)[:, None]
    indices, values = terms
    return sum(
        jnp.where(cells == indices[i][None], values[i][None], 0.0) for i in range(len(indices))
    )


def shards(covariance, courant, upwind, observed, noise):
    row_count, col_count = covariance.shape
    row_size, col_size = lax.axis_size("row"), lax.axis_size("col")
    row_pos, col_pos = lax.axis_index("row"), lax.axis_index("col")
    row_start, col_start = row_pos * row_count, col_pos * col_count
    side = math.isqrt(upwind.shape[0])
    coefs = stencil_coefs(courant, upwind, side)
    row_coefs = lax.dynamic_slice_in_dim(coefs, row_start, row_count + 2 * side, 1)
    col_coefs = lax.dynamic_slice_in_dim(coefs, col_start, col_count + 2 * side, 1)

    forward = [(i, i + 1) for i in range(row_size - 1)]
    backward = [(target, source) for source, target in forward]
    low = lax.ppermute(covariance[row_count - 2 * side :], "row", forward)

    table = jnp.concatenate([courant, upwind.astype(jnp.float32)[None]])
    depth = observed.shape[1]
    indices, values = expand(
        observed.reshape(1, -1), jnp.ones_like(noise).reshape(1, -1), table, side
    )
    one = indices[:, :depth], values[:, :depth]
    two = expand(indices[:, depth:], values[:, depth:], table, side)

    def observing(start, count):
        return jnp.concatenate([dense(one, start, count), dense(two, start, count)], axis=1)

    part = jnp.dot(covariance, observing(col_start, col_count), precision=HIGHEST)
    part, low, first_lines = lax.optimization_barrier((part, low, covariance[: 2 * side]))
    high = lax.ppermute(first_lines, "row", backward)
    chunk = lax.psum_scatter(part, "col", scatter_dimension=0, tiled=True)
    chunk_count = chunk.shape[0]
    mine = observing(row_start + col_pos * chunk_count, chunk_count)
    innov = lax.psum(jnp.dot(mine.T, chunk, precision=HIGHEST), ("row", "col"))
    innov = innov + jnp.diag(noise.reshape(-1))

    moves = []
    for source in range(row_size * col_size):
        moves.append((source, source % row_size * col_size + source // row_size))
    col_chunk = lax.ppermute(chunk, ("row", "col"), moves)
    row_panel = lax.all_gather(chunk, "col", axis=0, tiled=True)

    unit = jnp.eye(depth, dtype=innov.dtype)
    first_factor = jnp.linalg.cholesky(innov[:depth, :depth])
    first = jax.scipy.linalg.solve_triangular(first_factor, unit, lower=True)
    first, col_chunk = lax.optimization_barrier((first, col_chunk))
    col_panel = lax.all_gather(col_chunk, "row", axis=0, tiled=True)
    cross = jnp.dot(innov[depth:, :depth], first.T, precision=HIGHEST)
    rest = innov[depth:, depth:] - jnp.dot(cross, cross.T, precision=HIGHEST)
    factor, high = lax.optimization_barrier((jnp.linalg.cholesky(rest), high))
    block = left_twice(low, covariance, high, row_coefs, side)
    factor, block = lax.optimization_barrier((factor, block))
    low, high = shifted(block, "col", 1, 2 * side)
    second = jax.scipy.linalg.solve_triangular(factor, unit, lower=True)
    across = jnp.dot(second, jnp.dot(cross, first, precision=HIGHEST), precision=HIGHEST)
    inverse = jnp.concatenate(
        [
            jnp.concatenate([first, jnp.zeros_like(first)], axis=1),
            jnp.concatenate([-across, second], axis=1),
        ]
    )
    inverse, low, high = lax.optimization_barrier((inverse, low, high))
    row_ends = shifted(row_panel, "row", 0, 2 * side)
    col_ends = shifted(col_panel, "col", 0, 2 * side)
    block = right_twice(low, block, high, col_coefs, side)
    block, row_ends, col_ends = lax.optimization_barrier((block, row_ends, col_ends))
    row_panel = left_twice(row_ends[0], row_panel, row_ends[1], row_coefs, side)
    col_panel = left_twice(col_ends[0], col_panel, col_ends[1], col_coefs, side)
    row_panel = jnp.dot(row_panel, inverse.T, precision=HIGHEST)
    col_panel = lax.dot_general(
        inverse, col_panel, (((1,), (1,)), ((), ())), precision=HIGHEST
    )
    return subtract_product(block, row_panel, col_panel)


def solution(mesh):
    in_specs = (P("row", "col"), P(), P(), P(), P())
    out_specs = P("row", "col")
    return jax.shard_map(shards, mesh=mesh, in_specs=in_specs, out_specs=out_specs, check_vma=False)
```

time: 1530 us -> 908 us (0.59)
  other arithmetic: 529 us -> 117 us
  waiting for transfers between devices: 592 us -> 307 us
  local copies, waits for them, and re-layouts: 274 us -> 52.5 us
  Pallas kernels: 0 us -> 213 us
  starting transfers between devices: 21.2 us -> 92.5 us
    add x6 -> x7, other arithmetic: 267 us -> 6.79 us  [the longest x4 5.44 us: dense(): sum((jnp.where(cells == indices[i][None], values[i][None], 0.0) for i in...]
    psum x4 -> x1, waiting for transfers between devices: 416 us -> 169 us  [shards(): innov = lax.psum(jnp.dot(mine.T, chunk, precision=HIGHEST), ('row', 'col'))]
    pallas_call x0 -> x5, Pallas kernels: none -> 213 us  [the longest x1 75.3 us: subtract_product(): pl.pallas_call(functools.partial(subtract_kernel, min(512, width)), grid=...]
    concatenate x4 -> x3, other arithmetic: 130 us -> 0.25 us  [the longest x1 0.12 us: shards(): table = jnp.concatenate([courant, upwind.astype(jnp.float32)[None]])]
    reshape x4 -> x2, local copies, waits for them, and re-layouts: 129 us -> 0.16 us  [the longest x1 0.15 us: shards(): observed.reshape(1, -1)]
    ppermute x8 -> x9, waiting for transfers between devices: 176 us -> 91.3 us  [the longest x1 86.4 us: shards(): high = lax.ppermute(first_lines, 'row', backward)]
    ppermute x8 -> x9, starting transfers between devices: 20.8 us -> 92.4 us  [the longest x3 78.3 us: shifted(): lax.ppermute(lax.slice_in_dim(block, size - width, size, axis=dim), axis,...]
    gather x6 -> x2, local copies, waits for them, and re-layouts: 64.7 us -> 9.36 us  [expand(): jnp.take(table, index.reshape(-1), axis=1).reshape(3, *index.shape)]
  transfers between devices with their start and end apart: 12 -> 13, of which waited for: 11 -> 4; matrix products, arithmetic and copies ran while one was open for 2% -> 25% of each run, Pallas kernels for 0% -> 12%
where the time goes in v1:
time: 908 us; the launch traced here: 898 us
  waiting for transfers between devices  307 us (34%)
  Pallas kernels  213 us (23%)
  other arithmetic  117 us (13%)
  matrix products  98.1 us (11%)
  starting transfers between devices  92.5 us (10%)
  local copies, waits for them, and re-layouts  52.5 us (6%)
  between operations  16.9 us (2%)
    psum x1, waiting for transfers between devices, shards(): innov = lax.psum(jnp.dot(mine.T, chunk, precision=HIGHEST), ('row', 'col'))  169 us
    ppermute x1, waiting for transfers between devices, shards(): high = lax.ppermute(first_lines, 'row', backward)  86.4 us
    ppermute x3, starting transfers between devices, shifted(): lax.ppermute(lax.slice_in_dim(block, size - width, size, axis=dim), axis,...  78.3 us
    pallas_call x1, Pallas kernels, subtract_product(): pl.pallas_call(functools.partial(subtract_kernel, min(512, width)), grid=...  75.3 us
    pallas_call x3, Pallas kernels, left_twice(): pl.pallas_call(functools.partial(left_kernel, side), grid=(width // tile,...  71.9 us
    pallas_call x1, Pallas kernels, right_twice(): pl.pallas_call(functools.partial(right_kernel, side), grid=(rows // tile,...  66.1 us
    dot_general x1, matrix products, shards(): jnp.dot(covariance, observing(col_start, col_count), precision=HIGHEST)  60.9 us
    reduce_scatter x1, waiting for transfers between devices, shards(): chunk = lax.psum_scatter(part, 'col', scatter_dimension=0, tiled=True)  46.1 us
  transfers between devices with their start and end apart: 13, of which 4 were waited for; matrix products, arithmetic and copies ran while one was open for 25% of the time, Pallas kernels for 12%

profile of v1, /device:TPU:0, one launch (start us, length us, event | category | flops | bytes accessed | tf_op | source)
XLA Modules:
  0.0 897.9 jit_solution(15681246169478781982)
XLA Ops:
  6.5 7.7 fusion.58
  14.2 6.8 collective-permute-start
  21.3 5.1 copy.36
  43.5 60.9 %fusion.4 = f32[2048,512]{1,0:T(8,128)} fusion(f32[2048,4096]{1,0:T(8,128)} %mid_ref.1, f32[4096,256]{1,0:T(8,128)S(1)} %select_add_fusion, f32[4096,256]{1,0:T(8,128)S(1)} %select_add_fusion.1), kind=kOutput, calls=%fused_computation.12 | convolution fusion | flops 51541704704 | bytes 46137344 | tf_op jit(solution)/shard_map/dot_general | solution.py:275
  110.1 46.1 %reduce-scatter.2.cloned.1.call-done = f32[512,512]{1,0:T(8,128)} async-done(((f32[2048,512]{1,0:T(8,128)}), f32[512,512]{1,0:T(8,128)}) %reduce-scatter.2.cloned.1.call-update) | async-done | bytes 1048592 | tf_op jit(solution)/shard_map/reduce_scatter | solution.py:278
  163.3 169.2 %all-reduce.5.cloned.1.call-done = f32[512,512]{0,1:T(8,128)} async-done(((f32[512,512]{0,1:T(8,128)}), f32[512,512]{0,1:T(8,128)}) %all-reduce.5.cloned.1.call-update) | async-done | bytes 1048592 | tf_op jit(solution)/shard_map/psum | solution.py:281
  334.0 11.7 %cholesky.130 = f32[128,128]{1,0:T(8,128)S(1)} custom-call(f32[128,128]{1,0:T(8,128)S(1)} %cholesky.194), custom_call_target="Cholesky" | custom-call | tf_op jit(solution)/shard_map/jit(cholesky)/cholesky | solution.py:291
  345.8 9.8 %custom-call.13 = f32[1,128,128]{1,2,0:T(8,128)S(1)} custom-call(f32[1,128,128]{2,1,0:T(8,128)S(1)} %get-tuple-element.115), custom_call_target="InvertDiagBlocksLowerTriangular" | custom-call | tf_op jit(solution)/shard_map/jit(cholesky)/cholesky | solution.py:291
  356.1 11.7 %cholesky.147 = f32[128,128]{1,0:T(8,128)S(1)} custom-call(f32[128,128]{1,0:T(8,128)S(1)} %convolution_subtract_fusion.4), custom_call_target="Cholesky" | custom-call | tf_op jit(solution)/shard_map/jit(cholesky)/cholesky | solution.py:291
  374.8 19.7 %custom-call.14 = f32[2,128,128]{1,2,0:T(8,128)S(1)} custom-call(f32[2,128,128]{2,1,0:T(8,128)S(1)} %get-tuple-element.55), custom_call_target="InvertDiagBlocksLowerTriangular" | custom-call | tf_op jit(solution)/shard_map/jit(_solve_triangular)/triangular_solve | solution.py:292
  399.0 11.7 %cholesky.164 = f32[128,128]{1,0:T(8,128)S(1)} custom-call(f32[128,128]{1,0:T(8,128)S(1)} %cholesky.197), custom_call_target="Cholesky" | custom-call | tf_op jit(solution)/shard_map/jit(cholesky)/cholesky | solution.py:297
  410.7 9.8 %custom-call.15 = f32[1,128,128]{1,2,0:T(8,128)S(1)} custom-call(f32[1,128,128]{2,1,0:T(8,128)S(1)} %get-tuple-element.111), custom_call_target="InvertDiagBlocksLowerTriangular" | custom-call | tf_op jit(solution)/shard_map/jit(cholesky)/cholesky | solution.py:297
  421.0 11.7 %cholesky.181 = f32[128,128]{1,0:T(8,128)S(1)} custom-call(f32[128,128]{1,0:T(8,128)S(1)} %convolution_subtract_fusion.3), custom_call_target="Cholesky" | custom-call | tf_op jit(solution)/shard_map/jit(cholesky)/cholesky | solution.py:297
  435.4 86.4 %collective-permute-done.2.high_ref = f32[256,4096]{1,0:T(8,128)} collective-permute-done((f32[256,4096]{1,0:T(8,128)}, f32[256,4096]{1,0:T(8,128)}, u32[]{:S(2)}, u32[]{:S(2)}) %collective-permute-start.2) | collective-permute-done | bytes 4194336 | tf_op jit(solution)/shard_map/ppermute | solution.py:277
  525.6 43.8 %shard_map.55.mid_ref = f32[2048,4096]{1,0:T(8,128)} custom-call(f32[256,4096]{1,0:T(8,128)} %collective-permute-done.low_ref, f32[2048,4096]{1,0:T(8,128)} %mid_ref.1, f32[256,4096]{1,0:T(8,128)} %collective-permute-done.2.high_ref, f32[5,2304,128]{2,1,0:T(8,128)} %broadcast_in_dim.357.coef_ref), custom_call_target="tpu_custom_call" | custom-call | flops 301989888 | bytes 67108864 | tf_op jit(solution)/shard_map/pallas_call | solution.py:126
  580.9 19.7 %custom-call.16 = f32[2,128,128]{1,2,0:T(8,128)S(1)} custom-call(f32[2,128,128]{2,1,0:T(8,128)S(1)} %get-tuple-element.56), custom_call_target="InvertDiagBlocksLowerTriangular" | custom-call | tf_op jit(solution)/shard_map/jit(_solve_triangular)/triangular_solve | solution.py:301
  604.5 73.4 %collective-permute-start.5 = (f32[256,512]{1,0:T(8,128)}, f32[256,512]{1,0:T(8,128)}, u32[]{:S(2)}, u32[]{:S(2)}) collective-permute-start(f32[256,512]{1,0:T(8,128)} %get-tuple-element.94), channel_id=1, source_target_pairs={{0,4},{4,8},{8,12},{12,16},{16,20},{20,24},{24,28},{1,5},{5,9},{9,... | collective-permute-start | bytes 1572872 | tf_op jit(solution)/shard_map/ppermute | solution.py:20
  687.9 66.1 %shard_map.56.block_ref = f32[2048,4096]{1,0:T(8,128)} custom-call(f32[2048,256]{1,0:T(8,128)} %copy-done.1, f32[2048,4096]{1,0:T(8,128)} %shard_map.55.mid_ref, f32[2048,256]{1,0:T(8,128)} %collective-permute-done.4.high_ref, f32[5,8,4352]{2,1,0:T(8,128)} %broadcast_in_dim.358.coef_ref), custom_call_target="tpu_custom_call" | custom-call | flops 301989888 | bytes 67108864 | tf_op jit(solution)/shard_map/pallas_call | solution.py:153
  754.0 6.5 broadcast_in_dim.359.coef_ref
  760.6 18.0 %shard_map.58 = f32[4096,512]{1,0:T(8,128)} custom-call(f32[256,512]{1,0:T(8,128)} %copy-done.2, f32[4096,512]{1,0:T(8,128)} %all-gather.5.cloned.1.call-done.mid_ref, f32[256,512]{1,0:T(8,128)} %copy-done.3, f32[5,4352,128]{2,1,0:T(8,128)} %broadcast_in_dim.359.coef_ref), custom_call_target="tpu_custom_call" | custom-call | flops 75497472 | bytes 16777216 | tf_op jit(solution)/shard_map/pallas_call | solution.py:126
  778.6 17.2 %fusion.70.right_ref = f32[512,4096]{1,0:T(8,128)} fusion(f32[512,512]{1,0:T(8,128)S(1)} %select_maximum_fusion, f32[4096,512]{1,0:T(8,128)} %shard_map.58), kind=kOutput, calls=%fused_computation.176 | convolution fusion | flops 12884901888 | bytes 17825792 | tf_op jit(solution)/shard_map/dot_general | solution.py:317
  795.8 10.1 %shard_map.57 = f32[2048,512]{1,0:T(8,128)} custom-call(f32[256,512]{1,0:T(8,128)} %collective-permute-done.5.low_ref, f32[2048,512]{1,0:T(8,128)} %all-gather.3.cloned.1.call-done.mid_ref, f32[256,512]{1,0:T(8,128)} %collective-permute-done.6.high_ref, f32[5,2304,128]{2,1,0:T(8,128)} %broadcast_in_dim.357.coef_ref), custom_call_target="tpu_custom_call" | custom-call | flops 37748736 | bytes 8388608 | tf_op jit(solution)/shard_map/pallas_call | solution.py:126
  805.9 9.8 %fusion.69.left_ref = f32[2048,512]{1,0:T(8,128)} fusion(f32[2048,512]{1,0:T(8,128)} %shard_map.57, f32[512,512]{1,0:T(8,128)S(1)} %select_maximum_fusion), kind=kOutput, calls=%fused_computation.175 | convolution fusion | flops 6442450944 | bytes 9437184 | tf_op jit(solution)/shard_map/dot_general | solution.py:316
  815.7 75.3 %shard_map.59 = f32[2048,4096]{1,0:T(8,128)} custom-call(f32[2048,4096]{1,0:T(8,128)} %shard_map.56.block_ref, f32[2048,512]{1,0:T(8,128)} %fusion.69.left_ref, f32[512,4096]{1,0:T(8,128)} %fusion.70.right_ref), custom_call_target="tpu_custom_call" | custom-call | flops 51539607552 | bytes 67108864 | tf_op jit(solution)/shard_map/pallas_call | solution.py:193
  (160 shorter events, 81.0 us)
Async XLA Ops:
  6.5 14.5 %copy-start.8 = (s32[2,256]{1,0:T(2,128)S(1)}, s32[2,256]{1,0:T(2,128)}, u32[]{:S(2)}) copy-start(s32[2,256]{1,0:T(2,128)} %param.11) | copy-start | bytes 6148
  6.5 14.6 %copy-start.6 = (s32[16384]{0:T(1024)S(1)}, s32[16384]{0:T(1024)}, u32[]{:S(2)}) copy-start(s32[16384]{0:T(1024)} %param.10) | copy-start | bytes 196612
  6.5 14.7 %copy-start.4 = (f32[2,16384]{1,0:T(2,128)S(1)}, f32[2,16384]{1,0:T(2,128)}, u32[]{:S(2)}) copy-start(f32[2,16384]{1,0:T(2,128)} %param.9) | copy-start | bytes 393220
  6.5 149.6 %reduce-scatter.2.cloned.1.call-start = ((), (), s32[]{:S(2)}) async-start(), calls=%async_computation.1 | async-start | bytes 5242880 | tf_op jit(solution)/shard_map/reduce_scatter | solution.py:278
  14.2 95.0 %collective-permute-start = (f32[256,4096]{1,0:T(8,128)}, f32[256,4096]{1,0:T(8,128)}, u32[]{:S(2)}, u32[]{:S(2)}) collective-permute-start(f32[256,4096]{1,0:T(8,128)} %get-tuple-element.90), channel_id=1, source_target_pairs={{0,4},{4,8},{8,12},{12,16},{16,20},{20,24},{24,28},{1,5},{5,9},{9,... | collective-permute-start | bytes 12582920 | tf_op jit(solution)/shard_map/ppermute | solution.py:262
  109.2 51.8 %copy-start.9 = (f32[2,256]{1,0:T(2,128)S(1)}, f32[2,256]{1,0:T(2,128)}, u32[]{:S(2)}) copy-start(f32[2,256]{1,0:T(2,128)} %param.12) | copy-start | bytes 6148
  109.3 223.2 %all-reduce.5.cloned.1.call-start = ((), (), s32[]{:S(2)}) async-start(), calls=%async_computation.2 | async-start | bytes 2097152 | tf_op jit(solution)/shard_map/psum | solution.py:281
  156.1 5.0 copy-start
  160.3 441.9 %all-gather.3.cloned.1.call-start = ((), (), s32[]{:S(2)}) async-start(), calls=%async_computation.3 | async-start | bytes 5242880 | tf_op jit(solution)/shard_map/all_gather | solution.py:288
  161.0 518.2 %all-gather.5.cloned.1.call-start = ((), (), s32[]{:S(2)}) async-start(), calls=%async_computation.4 | async-start | bytes 9437184 | tf_op jit(solution)/shard_map/all_gather | solution.py:294
  161.1 234.2 %collective-permute-start.1 = (f32[512,512]{1,0:T(8,128)S(1)}, f32[512,512]{1,0:T(8,128)}, u32[]{:S(2)}, u32[]{:S(2)}) collective-permute-start(f32[512,512]{1,0:T(8,128)S(1)} %copy-done), channel_id=1, source_target_pairs={{0,0},{1,4},{2,8},{3,12},{4,16},{5,20},{6,24},{7,28},{8,1},{9,5},{... | collective-permute-start | bytes 3145736 | tf_op jit(solution)/shard_map/ppermute | solution.py:287
  395.4 126.4 %collective-permute-start.2 = (f32[256,4096]{1,0:T(8,128)}, f32[256,4096]{1,0:T(8,128)}, u32[]{:S(2)}, u32[]{:S(2)}) collective-permute-start(f32[256,4096]{1,0:T(8,128)} %get-tuple-element.26), channel_id=1, source_target_pairs={{4,0},{8,4},{12,8},{16,12},{20,16},{24,20},{28,24},{5,1},{9,5},{13... | collective-permute-start | bytes 12582920 | tf_op jit(solution)/shard_map/ppermute | solution.py:277
  574.0 110.0 %collective-permute-start.3 = (f32[2048,256]{1,0:T(8,128)}, f32[2048,256]{1,0:T(8,128)S(1)}, u32[]{:S(2)}, u32[]{:S(2)}) collective-permute-start(f32[2048,256]{1,0:T(8,128)} %get-tuple-element.88), channel_id=1, source_target_pairs={{0,1},{1,2},{2,3},{4,5},{5,6},{6,7},{8,9},{9,10},{10,11},{12,13},{... | collective-permute-start | bytes 6291464 | tf_op jit(solution)/shard_map/ppermute | solution.py:20
  575.4 111.6 %collective-permute-start.4 = (f32[2048,256]{1,0:T(8,128)}, f32[2048,256]{1,0:T(8,128)}, u32[]{:S(2)}, u32[]{:S(2)}) collective-permute-start(f32[2048,256]{1,0:T(8,128)} %get-tuple-element.87), channel_id=1, source_target_pairs={{1,0},{2,1},{3,2},{5,4},{6,5},{7,6},{9,8},{10,9},{11,10},{13,12},{... | collective-permute-start | bytes 6291464 | tf_op jit(solution)/shard_map/ppermute | solution.py:21
  600.6 83.5 %copy-start.7 = (f32[2,128,128]{1,2,0:T(8,128)}, f32[2,128,128]{1,2,0:T(8,128)S(1)}, u32[]{:S(2)}) copy-start(f32[2,128,128]{1,2,0:T(8,128)S(1)} %custom-call.16) | copy-start | bytes 393220
  601.8 83.5 %copy-start.5 = (f32[128,256]{1,0:T(8,128)S(1)}, f32[128,256]{1,0:T(8,128)}, u32[]{:S(2)}) copy-start(f32[128,256]{1,0:T(8,128)} %convolution_subtract_fusion.1) | copy-start | bytes 393220
  604.5 149.5 %collective-permute-start.5 = (f32[256,512]{1,0:T(8,128)}, f32[256,512]{1,0:T(8,128)}, u32[]{:S(2)}, u32[]{:S(2)}) collective-permute-start(f32[256,512]{1,0:T(8,128)} %get-tuple-element.94), channel_id=1, source_target_pairs={{0,4},{4,8},{8,12},{12,16},{16,20},{20,24},{24,28},{1,5},{5,9},{9,... | collective-permute-start | bytes 1572872 | tf_op jit(solution)/shard_map/ppermute | solution.py:20
  677.9 76.1 %collective-permute-start.6 = (f32[256,512]{1,0:T(8,128)}, f32[256,512]{1,0:T(8,128)}, u32[]{:S(2)}, u32[]{:S(2)}) collective-permute-start(f32[256,512]{1,0:T(8,128)} %get-tuple-element.93), channel_id=1, source_target_pairs={{4,0},{8,4},{12,8},{16,12},{20,16},{24,20},{28,24},{5,1},{9,5},{13... | collective-permute-start | bytes 1572872 | tf_op jit(solution)/shard_map/ppermute | solution.py:21
  680.5 73.5 %collective-permute-start.7 = (f32[256,512]{1,0:T(8,128)S(1)}, f32[256,512]{1,0:T(8,128)S(1)}, u32[]{:S(2)}, u32[]{:S(2)}) collective-permute-start(f32[256,512]{1,0:T(8,128)S(1)} %get-tuple-element.92), channel_id=1, source_target_pairs={{0,1},{1,2},{2,3},{4,5},{5,6},{6,7},{8,9},{9,10},{10,11},{12,13},{... | collective-permute-start | bytes 1572872 | tf_op jit(solution)/shard_map/ppermute | solution.py:20
  684.0 3.9 copy-start.1
  684.0 70.0 %collective-permute-start.8 = (f32[256,512]{1,0:T(8,128)S(1)}, f32[256,512]{1,0:T(8,128)S(1)}, u32[]{:S(2)}, u32[]{:S(2)}) collective-permute-start(f32[256,512]{1,0:T(8,128)S(1)} %get-tuple-element.91), channel_id=1, source_target_pairs={{1,0},{2,1},{3,2},{5,4},{6,5},{7,6},{9,8},{10,9},{11,10},{13,12},{... | collective-permute-start | bytes 1572872 | tf_op jit(solution)/shard_map/ppermute | solution.py:21
  754.0 6.5 copy-start.2
  754.0 6.5 copy-start.3
Sparse Core Ops, SparseCore 0:
  109.4 46.7 reduce-scatter.1
  162.1 170.2 all-reduce.4
  334.0 33.5 all-gather.2
  395.5 189.0 all-gather.4
